TPU v7x, 32 devices: a whole 2x2x4 slice. The times are simulated.
32 devices in a mesh: grp: 4 (over x, core), dev: 8 (over z, y).
Axes of the slice: x: 2, y: 2, z: 4, core: 2. Of those that a mesh axis runs over, the one named last changes fastest.
Arguments:
- voltages: bfloat16 [512, 16384], P(('grp', 'dev')), may hold values from -6 to 6
- filter_taps: float32 [4, 4096], replicated, may hold values from -0.046875 to 0.046875
- dipole_cells: int32 [512, 2], replicated, may hold values from 0 to 254
- kernel_bits: int32 [512, 2], replicated, may hold values from 1 to 3
- sky_model: float32 [2048, 256, 256], P('grp', 'dev'), may hold values from 0 to 2
Outputs:
- residual_images: float32 [2048, 256, 256], P('grp', 'dev')
- broadband: float32 [256, 256], P('dev')
Inputs may be any that keep to these rules, and one draw needn't show every extreme that they name: `dipole_cells`: grid row and column of a dipole's first kernel cell; the kernel may also reach index plus one. `kernel_bits`: bit 0 gives weight 1 to the cell at the index, bit 1 to the cell at the index plus one.
All inputs are finite; a program needn't handle non-finite values.
Results may differ from a plain program's by a relative error of at most 0.005.
Values may be sent and summed in bfloat16 or wider, within the bound.
A program may use at most 192 MiB of HBM per device.

v0:
```python
import math

import jax
import jax.numpy as jnp
from jax import lax
from jax.sharding import PartitionSpec as P


def spectrum_table(points, channels):
    sample_idx = lax.broadcasted_iota(jnp.int32, (points, channels), 0)
    channel_idx = lax.broadcasted_iota(jnp.int32, (points, channels), 1)
    angle = (sample_idx * channel_idx % points).astype(jnp.float32) * (2.0 * math.pi / points)
    return jnp.stack([jnp.cos(angle), -jnp.sin(angle)])


def transform_table(length):
    out_idx = lax.broadcasted_iota(jnp.int32, (length, length), 0)
    in_idx = lax.broadcasted_iota(jnp.int32, (length, length), 1)
    angle = (out_idx * in_idx % length).astype(jnp.float32) * (2.0 * math.pi / length)
    cosine = jnp.cos(angle)
    sine = jnp.sin(angle)
    return jnp.stack([jnp.stack([cosine, sine]), jnp.stack([-sine, cosine])])


def split_table(table):
    upper_part = table.astype(jnp.bfloat16)
    lower_part = (table - upper_part.astype(jnp.float32)).astype(jnp.bfloat16)
    return (upper_part, lower_part)


def one_hot(cell_col, bit_col, length):
    rows_iota = lax.broadcasted_iota(jnp.int32, (length, cell_col.shape[0]), 0)
    lower = (rows_iota == cell_col[None, :]) * (bit_col % 2)[None, :]
    upper = (rows_iota == cell_col[None, :] + 1) * (bit_col // 2)[None, :]
    return (lower + upper).astype(jnp.bfloat16)


def group_major(values, groups, members):
    width = values.shape[1]
    return values.reshape(groups, members, -1, width).transpose(1, 0, 2, 3).reshape(values.shape)


def channelize(voltages, filter_taps):
    tap_count, points = filter_taps.shape
    dipoles = voltages.shape[0]
    segments = voltages.reshape(dipoles, -1, points)
    frame_count = segments.shape[1] - tap_count + 1
    framed = jnp.zeros((dipoles, frame_count, points), jnp.float32)
    for tap_index in range(tap_count):
        framed = framed + filter_taps[tap_index][None, None, :] * segments[
            :, tap_index : tap_index + frame_count, :
        ].astype(jnp.float32)
    table = spectrum_table(points, points // 2)
    spectra = jnp.einsum("afn,qnk->qfka", framed, table, precision=lax.Precision.HIGHEST)
    return spectra.astype(jnp.bfloat16)


def block_length(channels, row_bytes, target):
    length = 1
    while (
        length * 2 <= channels
        and channels % (length * 2) == 0
        and (length * 2 * row_bytes <= target)
    ):
        length = length * 2
    return length


def grid_half(spectra, row_kernel, col_kernel, w_table):
    parts, frame_count, channels, dipoles = spectra.shape
    col_count = col_kernel.shape[0]
    grid_len = row_kernel.shape[0]
    span = block_length(channels, 4 * frame_count * col_count * dipoles, 2**22)
    blocks = channels // span
    portions = spectra.reshape(parts, frame_count, blocks, span, dipoles).transpose(2, 0, 1, 3, 4)

    def single(portion):
        spread = portion[:, :, :, None, :] * col_kernel[None, None, None, :, :]
        aperture = jnp.einsum(
            "qfcva,ua->qfcvu", spread, row_kernel, preferred_element_type=jnp.float32
        )
        half_turn = jnp.einsum(
            "pqUu,qfcvu->pfcvU", w_table, aperture, precision=lax.Precision.HIGHEST
        )
        return half_turn.astype(jnp.bfloat16)

    halves = lax.map(single, portions)
    return halves.transpose(1, 2, 0, 3, 4, 5).reshape(
        parts, frame_count, channels, col_count, grid_len
    )


def image_power(half_turn, table_upper, table_lower, norm_scale, form):
    sky_image = jnp.einsum(form, table_upper, half_turn, preferred_element_type=jnp.float32)
    sky_image = sky_image + jnp.einsum(
        form, table_lower, half_turn, preferred_element_type=jnp.float32
    )
    return jnp.sum(sky_image * sky_image, axis=(0, 1)) * norm_scale


def body(voltages, filter_taps, dipole_cells, kernel_bits, sky_model):
    groups = lax.axis_size("grp")
    members = lax.axis_size("dev")
    dipoles = dipole_cells.shape[0]
    grid_len = sky_model.shape[2]
    rows_mine = sky_model.shape[1]
    spectra = channelize(voltages, filter_taps)
    w_table = transform_table(grid_len)
    table_upper, table_lower = split_table(w_table)
    norm_scale = 1.0 / (spectra.shape[1] * dipoles)
    turned = lax.all_to_all(spectra, "grp", split_axis=2, concat_axis=3, tiled=True)
    everyone = lax.all_gather(turned, "dev", axis=3, tiled=True)
    order_cells = group_major(dipole_cells, groups, members)
    order_bits = group_major(kernel_bits, groups, members)
    row_kernel = one_hot(order_cells[:, 0], order_bits[:, 0], grid_len)
    col_full = one_hot(order_cells[:, 1], order_bits[:, 1], grid_len)
    col_mine = lax.dynamic_slice_in_dim(col_full, lax.axis_index("dev") * rows_mine, rows_mine, 0)
    half_turn = grid_half(everyone, row_kernel, col_mine, w_table)
    power_sum = image_power(
        lax.all_to_all(half_turn, "dev", split_axis=4, concat_axis=3, tiled=True),
        table_upper,
        table_lower,
        norm_scale,
        "tksw,khnwm->thnms",
    )
    residual_images = power_sum - sky_model
    channel_total = residual_images.shape[0] * groups
    broadband = lax.psum(jnp.sum(residual_images, axis=0), "grp") / channel_total
    return (residual_images, broadband)


def solution(mesh):
    in_specs = (P(("grp", "dev"), None), P(), P(), P(), P("grp", "dev", None))
    out_specs = (P("grp", "dev", None), P("dev", None))
    return jax.shard_map(body, mesh=mesh, in_specs=in_specs, out_specs=out_specs, check_vma=False)
```

profile of v0, /device:TPU:0, one launch (start us, length us, event | category | flops | bytes accessed | tf_op | source)
XLA Modules:
  0.0 870.3 jit_solution(18061833683314547483)
XLA Ops:
  7.2 133.6 %sine_negate_fusion = (f32[1,4096,2048]{2,1,0:T(8,128)}, f32[1,4096,2048]{2,1,0:T(8,128)}) fusion(), kind=kLoop, calls=%fused_computation.36 | loop fusion | flops 125829120 | bytes 67108864 | tf_op jit(solution)/shard_map/neg | solution.py:13
  142.4 39.7 %fusion.38 = bf16[2,1,2048,16]{2,3,0,1:T(8,128)(2,1)S(1)} fusion(f32[1,4096,2048]{2,1,0:T(8,128)} %get-tuple-element.148, f32[1,4096,2048]{2,1,0:T(8,128)} %get-tuple-element.149, bf16[16,1,4096]{2,1,0:T(2,128)(2,1)S(1)} %get-tuple-element.133, bf16[16,1,4096]{2,1,0:T(2,128)(2,1)S(1)} %get-tuple-element.131, ...), kind=kOutput, calls=%fused_computation.43 | convolution fusion | flops 3238789120 | bytes 67829760 | tf_op jit(solution)/shard_map/afn,qnk->qfka/dot_general | solution.py:54
  184.6 4.2 all-to-all-start
  189.2 4.2 all-to-all-done
  197.9 38.9 %all-gather.2.cloned.1.call-done = bf16[2,1,512,512]{2,3,0,1:T(8,128)(2,1)} async-done(((bf16[2,1,512,64]{2,3,0,1:T(8,128)(2,1)}), bf16[2,1,512,512]{2,3,0,1:T(8,128)(2,1)}) %all-gather.2.cloned.1.call-update) | async-done | bytes 1048592 | tf_op jit(solution)/shard_map/all_gather | solution.py:112
  238.3 80.0 %while.11 = (s32[]{:T(128)}, bf16[8,2,1,64,32,256]{5,4,3,0,1,2:T(8,128)(2,1)}, bf16[8,2,1,64,512]{4,3,0,1,2:T(8,128)(2,1)S(1)}, bf16[32,512]{1,0:T(8,128)(2,1)S(...) while((s32[]{:T(128)}, ...), condition=%wide.region_1.2_spmd.clone, body=%wide.region_0.1_spmd.clone.sunk | while | flops 7520124928 | bytes 16425577 | solution.py:87
  239.8 7.0 fusion.99
  249.8 7.0 fusion.99
  259.8 7.0 fusion.99
  269.8 7.0 fusion.99
  279.8 7.0 fusion.99
  289.8 7.0 fusion.99
  299.8 7.0 fusion.99
  309.8 7.0 fusion.99
  318.3 30.6 %copy.86 = bf16[2,1,512,32,256]{2,3,1,0,4:T(8,128)(2,1)} copy(bf16[2,1,512,32,256]{4,3,2,0,1:T(8,128)(2,1)} %bitcast.111) | data formatting | bytes 33554432 | tf_op jit(solution)/shard_map/reshape | solution.py:88
  348.9 367.0 %all_to_all.33 = bf16[2,1,512,32,256]{2,3,1,0,4:T(8,128)(2,1)S(1)} all-to-all(bf16[2,1,512,32,256]{2,3,1,0,4:T(8,128)(2,1)} %copy.86), channel_id=1, replica_groups=mesh['grp'=4,'dev'=8] {'dev'}, dimensions={4} | all-to-all | bytes 33554432 | tf_op jit(solution)/shard_map/all_to_all | solution.py:120
  716.0 21.7 %copy.87 = bf16[2,1,512,32,256]{2,4,3,0,1:T(8,128)(2,1)S(1)} copy(bf16[2,1,512,32,256]{2,3,1,0,4:T(8,128)(2,1)S(1)} %all_to_all.33) | data formatting | bytes 33554432 | tf_op jit(solution)/shard_map/all_to_all | solution.py:120
  737.6 7.1 copy.88
  744.8 26.2 %copy.95 = bf16[2,512,256,32,1]{2,1,0,4,3:T(8,128)(2,1)} copy(bf16[2,512,256,32,1]{1,3,2,0,4:T(8,128)(2,1)} %bitcast.110) | data formatting | bytes 33554432 | tf_op jit(solution)/shard_map/reshape.23
  770.9 21.1 %fusion.43 = f32[512,32,2,256,1]{3,0,4,2,1:T(8,128)} fusion(bf16[2,512,256,32,1]{2,1,0,4,3:T(8,128)(2,1)} %copy.95, f32[1,2,256,256]{3,2,1,0:T(8,128)S(1)} %get-tuple-element.135, f32[1,2,256,256]{3,2,1,0:T(8,128)S(1)} %get-tuple-element.134), kind=kOutput, calls=%fused_computation.49 | convolution fusion | flops 8590983168 | bytes 51380224 | tf_op jit(solution)/shard_map/tksw,khnwm->thnms/dot_general | solution.py:94
  792.0 25.3 %fusion.30 = f32[512,32,256]{2,0,1:T(8,128)} fusion(f32[512,32,2,256,1]{3,0,4,2,1:T(8,128)} %fusion.43, bf16[2,512,256,32,1]{2,1,0,4,3:T(8,128)(2,1)} %copy.95, f32[1,2,256,256]{3,2,1,0:T(8,128)S(1)} %get-tuple-element.135, f32[1,2,256,256]{3,2,1,0:T(8,128)S(1)} %get-tuple-element.134), kind=kOutput, calls=%fused_computation.35 | convolution fusion | flops 8612216832 | bytes 68157440 | tf_op jit(solution)/shard_map/tksw,khnwm->thnms/dot_general | solution.py:95
  817.3 13.9 %fusion.81 = (f32[32,256]{1,0:T(8,128)S(1)}, f32[512,32,256]{2,0,1:T(8,128)S(1)}) fusion(f32[512,32,256]{2,1,0:T(8,128)} %param.11, f32[512,32,256]{2,0,1:T(8,128)} %fusion.30), kind=kLoop, calls=%fused_computation.111 | loop fusion | flops 12574720 | bytes 50364416 | tf_op jit(solution)/shard_map/reduce_sum | solution.py:128
  831.3 21.3 %copy.92 = f32[512,32,256]{2,1,0:T(8,128)} copy(f32[512,32,256]{2,0,1:T(8,128)S(1)} %get-tuple-element.129) | data formatting | bytes 33554432
  852.6 10.3 %psum.7 = f32[32,256]{1,0:T(8,128)S(1)} all-reduce(f32[32,256]{1,0:T(8,128)S(1)} %get-tuple-element.128), channel_id=1, replica_groups=mesh['grp'=4,'dev'=8] {'grp'}, use_global_device_ids=true, to_apply=%region_4.5 | all-reduce | flops 8192 | bytes 65536 | tf_op jit(solution)/shard_map/psum | solution.py:128
  (69 shorter events, 34.8 us)
Async XLA Ops:
  7.2 133.7 %copy-start = (bf16[16,16384]{1,0:T(8,128)(2,1)S(1)}, bf16[16,16384]{1,0:T(8,128)(2,1)}, u32[]{:S(2)}) copy-start(bf16[16,16384]{1,0:T(8,128)(2,1)} %param.7) | copy-start | bytes 1572868
  7.2 135.2 %copy-start.1 = (f32[4,4096]{1,0:T(4,128)S(1)}, f32[4,4096]{1,0:T(4,128)}, u32[]{:S(2)}) copy-start(f32[4,4096]{1,0:T(4,128)} %param.8) | copy-start | bytes 196612
  142.4 46.4 %copy-start.2 = (s32[512,2]{0,1:T(2,128)S(1)}, s32[512,2]{0,1:T(2,128)}, u32[]{:S(2)}) copy-start(s32[512,2]{0,1:T(2,128)} %param.10) | copy-start | bytes 12292
  142.4 46.6 %copy-start.3 = (s32[512,2]{0,1:T(2,128)S(1)}, s32[512,2]{0,1:T(2,128)}, u32[]{:S(2)}) copy-start(s32[512,2]{0,1:T(2,128)} %param.9) | copy-start | bytes 12292
  184.6 8.8 %all-to-all-start = ((bf16[4,2,8192]{2,1,0:T(2,128)(2,1)}), bf16[4,2,8192]{2,1,0:T(2,128)(2,1)S(1)}, u32[]{:S(2)}, u32[]{:S(2)}) async-start(bf16[4,2,8192]{2,1,0:T(2,128)(2,1)} %reshape.325), calls=%async_computation | async-start | bytes 262144 | tf_op jit(solution)/shard_map/all_to_all | solution.py:111
  188.8 48.0 %all-gather.2.cloned.1.call-start = ((), (), s32[]{:S(2)}) async-start(), calls=%async_computation.2 | async-start | bytes 1179648 | tf_op jit(solution)/shard_map/all_gather | solution.py:112
Sparse Core Ops, SparseCore 0:
  195.7 41.0 all-gather.1
where the time goes:
time: 872 us; the launch traced here: 870 us
  blocking collectives  377 us (43%)
  matrix products  153 us (18%)
  other arithmetic  150 us (17%)
  local copies, waits for them, and re-layouts  128 us (15%)
  waiting for transfers between devices  43.1 us (5%)
  between operations  14.2 us (2%)
    all_to_all x1, blocking collectives, body(): lax.all_to_all(half_turn, 'dev', split_axis=4, concat_axis=3, tiled=True)  367 us
    neg x1, other arithmetic, spectrum_table(): return jnp.stack([jnp.cos(angle), -jnp.sin(angle)])  134 us
    dot_general x8, matrix products, single(): jnp.einsum('pqUu,qfcvu->pfcvU', w_table, aperture, precision=lax.Precisio...  55.9 us
    dot_general x1, matrix products, channelize(): jnp.einsum('afn,qnk->qfka', framed, table, precision=lax.Precision.HIGHEST)  39.7 us
    all_gather x1, waiting for transfers between devices, body(): everyone = lax.all_gather(turned, 'dev', axis=3, tiled=True)  38.9 us
    reshape x1, local copies, waits for them, and re-layouts, grid_half(): halves.transpose(1, 2, 0, 3, 4, 5)  30.6 us
    all_to_all x2, local copies, waits for them, and re-layouts, body(): lax.all_to_all(half_turn, 'dev', split_axis=4, concat_axis=3, tiled=True)  28.8 us
    another operation x1, local copies, waits for them, and re-layouts  26.2 us
  transfers between devices with their start and end apart: 2, of which 2 were waited for; matrix products, arithmetic and copies ran while one was open for 0% of the time, Pallas kernels for 0%

commit v1 on v0

v1 whole, which is shorter than its diff:
```python
import functools
import math

import jax
import jax.numpy as jnp
import numpy as np
from jax import lax
from jax.experimental import pallas as pl
from jax.experimental.pallas import tpu as pltpu
from jax.sharding import PartitionSpec as P


def stage_tables(points):
    first = 1 << (int(math.log2(points)) // 2)
    second = points // first
    k1 = np.arange(first)
    n2 = np.arange(second)
    k2 = np.arange(second // 2)
    inner = np.exp(-2j * np.pi * np.outer(k1, k1) / first)
    twiddle = np.exp(-2j * np.pi * np.outer(k1, n2) / points)
    outer = np.exp(-2j * np.pi * np.outer(k2, n2) / second)
    as_pair = lambda z: np.stack([z.real, z.imag]).astype(np.float32)
    return as_pair(inner), as_pair(twiddle), as_pair(outer)


def channelize(voltages, filter_taps):
    tap_count, points = filter_taps.shape
    dipoles = voltages.shape[0]
    segments = voltages.reshape(dipoles, -1, points)
    frame_count = segments.shape[1] - tap_count + 1
    framed = jnp.zeros((dipoles, frame_count, points), jnp.float32)
    for tap in range(tap_count):
        framed = framed + filter_taps[tap][None, None, :] * segments[
            :, tap : tap + frame_count, :
        ].astype(jnp.float32)
    inner, twiddle, outer = stage_tables(points)
    first, second = twiddle.shape[1:]
    grid = framed.reshape(dipoles, frame_count, first, second)
    mid = jnp.einsum("qkn,afnm->qafkm", inner, grid, precision=lax.Precision.HIGHEST)
    turned = jnp.stack(
        [
            mid[0] * twiddle[0] - mid[1] * twiddle[1],
            mid[0] * twiddle[1] + mid[1] * twiddle[0],
        ]
    )
    full = np.stack([np.stack([outer[0], -outer[1]]), np.stack([outer[1], outer[0]])])
    spectra = jnp.einsum("pqjm,qafkm->pfajk", full, turned, precision=lax.Precision.HIGHEST)
    return spectra.astype(jnp.bfloat16).reshape(2, frame_count, dipoles, points // 2)


def phase(product, length):
    angle = (product % length).astype(jnp.float32) * (2.0 * math.pi / length)
    return jnp.cos(angle), jnp.sin(angle)


def row_factors(cells, bits, first_row, rows, length, scale):
    out = first_row + lax.broadcasted_iota(jnp.int32, (rows, cells.shape[0]), 0)
    low = (bits % 2).astype(jnp.float32) * scale
    high = (bits // 2).astype(jnp.float32) * scale
    cos_low, sin_low = phase(out * cells[None, :], length)
    cos_high, sin_high = phase(out * (cells[None, :] + 1), length)
    return jnp.stack([low * cos_low + high * cos_high, -(low * sin_low + high * sin_high)])


def col_factors(cells, bits, length):
    half = length // 2
    low = (bits % 2).astype(jnp.float32)[:, None]
    high = (bits // 2).astype(jnp.float32)[:, None]
    lane = lax.broadcasted_iota(jnp.int32, (cells.shape[0], half), 1)
    cos_low, sin_low = phase(lane * cells[:, None], length)
    cos_high, sin_high = phase((lane * (cells[:, None] + 1)), length)
    real = low * cos_low + high * cos_high
    imag = -(low * sin_low + high * sin_high)
    parity = (1 - 2 * (cells % 2)).astype(jnp.float32)[:, None]
    middle = low * parity - high * parity
    imag = jnp.where(lane == 0, middle, imag)
    return jnp.concatenate([real, imag], axis=1).astype(jnp.bfloat16)


def image_kernel(chunk, s_ref, r_ref, t_ref, sky_ref, out_ref, sum_ref, x_ref):
    step = pl.program_id(0)
    block, rows, length = sky_ref.shape
    half = length // 2
    group = chunk * rows

    @pl.when(step == 0)
    def _():
        sum_ref[...] = jnp.zeros_like(sum_ref)

    lane = lax.broadcasted_iota(jnp.int32, (group, half), 1)
    mirror = (half - lane) % half
    ends = lane == 0
    table = t_ref[...]
    total_low = jnp.zeros((rows, half), jnp.float32)
    total_high = jnp.zeros((rows, half), jnp.float32)
    for c in range(block // chunk):
        slot = c % 2
        row_re = r_ref[0]
        row_im = r_ref[1]
        for i in range(chunk):
            k = c * chunk + i
            s_re = s_ref[0, k : k + 1, :]
            s_im = s_ref[1, k : k + 1, :]
            x_ref[slot, i * rows : (i + 1) * rows, :] = (s_re * row_re - s_im * row_im).astype(
                jnp.bfloat16
            )
            x_ref[slot, group + i * rows : group + (i + 1) * rows, :] = (
                s_re * row_im + s_im * row_re
            ).astype(jnp.bfloat16)
        y = jnp.dot(x_ref[slot], table, preferred_element_type=jnp.float32)
        re_cos, re_sin = y[:group, :half], y[:group, half:]
        im_cos, im_sin = y[group:, :half], y[group:, half:]
        own = re_cos * re_cos + im_cos * im_cos
        other = re_sin * re_sin + im_sin * im_sin
        cross = 2.0 * (re_cos * im_sin - im_cos * re_sin)
        both = own + other
        low = jnp.where(ends, own, both - cross)
        high = jnp.where(ends, other, both + cross)
        high = jnp.take_along_axis(high, mirror, axis=1, mode="promise_in_bounds")
        ks = slice(c * chunk, (c + 1) * chunk)
        low = low.reshape(chunk, rows, half) - sky_ref[ks, :, :half]
        high = high.reshape(chunk, rows, half) - sky_ref[ks, :, half:]
        out_ref[ks, :, :half] = low
        out_ref[ks, :, half:] = high
        total_low = total_low + jnp.sum(low, axis=0)
        total_high = total_high + jnp.sum(high, axis=0)
    sum_ref[:, :half] += total_low
    sum_ref[:, half:] += total_high


def image(spectra, row_table, col_table, sky_model):
    channels, rows, length = sky_model.shape
    dipoles = spectra.shape[2]
    block = min(channels, 32)
    chunk = min(block, 8)
    macs = channels * rows * 2 * dipoles * length
    return pl.pallas_call(
        functools.partial(image_kernel, chunk),
        grid=(channels // block,),
        in_specs=[
            pl.BlockSpec((2, block, dipoles), lambda i: (0, i, 0)),
            pl.BlockSpec((2, rows, dipoles), lambda i: (0, 0, 0)),
            pl.BlockSpec((dipoles, length), lambda i: (0, 0)),
            pl.BlockSpec((block, rows, length), lambda i: (i, 0, 0)),
        ],
        out_specs=[
            pl.BlockSpec((block, rows, length), lambda i: (i, 0, 0)),
            pl.BlockSpec((rows, length), lambda i: (0, 0)),
        ],
        out_shape=[
            jax.ShapeDtypeStruct(sky_model.shape, jnp.float32),
            jax.ShapeDtypeStruct((rows, length), jnp.float32),
        ],
        scratch_shapes=[pltpu.VMEM((2, 2 * chunk * rows, dipoles), jnp.bfloat16)],
        compiler_params=pltpu.CompilerParams(vmem_limit_bytes=40 * 2**20),
        cost_estimate=pl.CostEstimate(
            flops=2 * macs, bytes_accessed=8 * sky_model.size, transcendentals=0
        ),
    )(spectra, row_table, col_table, sky_model)


def group_major(values, groups, members):
    return values.reshape(groups, members, -1, 2).transpose(1, 0, 2, 3).reshape(values.shape)


def body(voltages, filter_taps, dipole_cells, kernel_bits, sky_model):
    groups = lax.axis_size("grp")
    members = lax.axis_size("dev")
    dipoles = dipole_cells.shape[0]
    mine = voltages.shape[0]
    channels, rows, length = sky_model.shape
    spectra = channelize(voltages, filter_taps)
    frame_count = spectra.shape[1]
    assert frame_count == 1
    blocks = spectra.reshape(2, mine, groups, channels).transpose(2, 0, 1, 3)
    turned = lax.all_to_all(blocks, "grp", split_axis=0, concat_axis=0, tiled=True)
    everyone = lax.all_gather(turned, "dev", axis=0, tiled=True)
    everyone = everyone.transpose(1, 3, 0, 2).reshape(2, channels, dipoles).astype(jnp.float32)
    cells = group_major(dipole_cells, groups, members)
    bits = group_major(kernel_bits, groups, members)
    scale = math.sqrt(1.0 / (frame_count * dipoles))
    first_row = lax.axis_index("dev") * rows
    row_table = row_factors(cells[:, 0], bits[:, 0], first_row, rows, length, scale)
    col_table = col_factors(cells[:, 1], bits[:, 1], length)
    residual, partial = image(everyone, row_table, col_table, sky_model)
    broadband = lax.psum(partial, "grp") / (channels * groups)
    return residual, broadband


def solution(mesh):
    in_specs = (P(("grp", "dev"), None), P(), P(), P(), P("grp", "dev", None))
    out_specs = (P("grp", "dev", None), P("dev", None))
    return jax.shard_map(body, mesh=mesh, in_specs=in_specs, out_specs=out_specs, check_vma=False)
```

time: 872 us -> 115 us (0.13)
  blocking collectives: 377 us -> 10.3 us
  matrix products: 153 us -> 3.47 us
  other arithmetic: 150 us -> 10.2 us
  local copies, waits for them, and re-layouts: 128 us -> 9.02 us
  Pallas kernels: 0 us -> 23.5 us
    all_to_all x1 -> x0, blocking collectives: 367 us -> none  [body(): lax.all_to_all(half_turn, 'dev', split_axis=4, concat_axis=3, tiled=True)]
    dot_general x19 -> x2, matrix products: 153 us -> 3.47 us  [the longest x1 1.86 us: channelize(): jnp.einsum('qkn,afnm->qafkm', inner, grid, precision=lax.Precision.HIGHEST)]
    neg x2 -> x0, other arithmetic: 135 us -> none  [the longest x1 134 us: spectrum_table(): return jnp.stack([jnp.cos(angle), -jnp.sin(angle)])]
    all_to_all x4 -> x1, local copies, waits for them, and re-layouts: 30.2 us -> 0.66 us  [body(): lax.all_to_all(blocks, 'grp', split_axis=0, concat_axis=0, tiled=True)]
    reshape x7 -> x6, local copies, waits for them, and re-layouts: 31 us -> 1.74 us  [group_major(): values.reshape(groups, members, -1, 2).transpose(1, 0, 2, 3)]
    another operation x1 -> x3, local copies, waits for them, and re-layouts: 26.2 us -> 1.07 us  [the longest x2 0.85 us: body(): blocks = spectra.reshape(2, mine, groups, channels).transpose(2, 0, 1, 3)]
    unnamed x11 -> x0, local copies, waits for them, and re-layouts: 23.7 us -> none
    pallas_call x0 -> x1, Pallas kernels: none -> 23.5 us  [image(): pl.pallas_call(functools.partial(image_kernel, chunk), grid=(channels //...]
  transfers between devices with their start and end apart: 2 -> 2, of which waited for: 2 -> 2; matrix products, arithmetic and copies ran while one was open for 0% -> 6% of each run, Pallas kernels for 0% -> 0%
where the time goes in v1:
time: 115 us; the launch traced here: 114 us
  waiting for transfers between devices  38.9 us (34%)
  Pallas kernels  23.5 us (20%)
  between operations  14.2 us (12%)
  blocking collectives  10.3 us (9%)
  other arithmetic  10.2 us (9%)
  local copies, waits for them, and re-layouts  9.02 us (8%)
  starting transfers between devices  4.21 us (4%)
  matrix products  3.47 us (3%)
    all_gather x1, waiting for transfers between devices, body(): everyone = lax.all_gather(turned, 'dev', axis=0, tiled=True)  35.2 us
    pallas_call x1, Pallas kernels, image(): pl.pallas_call(functools.partial(image_kernel, chunk), grid=(channels //...  23.5 us
    psum x1, blocking collectives, body(): broadband = lax.psum(partial, 'grp') / (channels * groups)  10.3 us
    another operation x2, other arithmetic  4.37 us
    all_to_all x1, starting transfers between devices, body(): lax.all_to_all(blocks, 'grp', split_axis=0, concat_axis=0, tiled=True)  4.21 us
    all_to_all x1, waiting for transfers between devices, body(): lax.all_to_all(blocks, 'grp', split_axis=0, concat_axis=0, tiled=True)  3.73 us
    convert_element_type x1, other arithmetic, body(): everyone.transpose(1, 3, 0, 2).reshape(2, channels, dipoles)  2.84 us
  transfers between devices with their start and end apart: 2, of which 2 were waited for; matrix products, arithmetic and copies ran while one was open for 6% of the time, Pallas kernels for 0%

profile of v1, /device:TPU:0, one launch (start us, length us, event | category | flops | bytes accessed | tf_op | source)
XLA Modules:
  0.0 113.7 jit_solution(8348835788040763825)
XLA Ops:
  7.2 1.1 fusion.38
  8.2 1.4 %reshape.490 = bf16[16,4,4096]{2,1,0:T(4,128)(2,1)S(1)} reshape(bf16[16,16384]{1,0:T(8,128)(2,1)} %param.11) | data formatting | bytes 1048576 | tf_op jit(solution)/shard_map/reshape | solution.py:29
  9.7 1.1 %fusion.37 = (bf16[16,1,4096]{2,1,0:T(2,128)(2,1)S(1)}, bf16[16,1,4096]{2,1,0:T(2,128)(2,1)S(1)}, bf16[16,1,4096]{2,1,0:T(2,128)(2,1)S(1)}, bf16[16,1,4096]{2,1,0:T(2,128)(2,1)S(1)}) fusion(bf16[16,4,4096]{2,1,0:T(4,128)(2,1)S(1)} %reshape.490), kind=kLoop, calls=%fused_computation.87 | loop fusion | bytes 1048576 | tf_op jit(solution)/shard_map/slice | solution.py:33
  10.8 0.7 multiply_add_fusion.1
  11.5 0.2 reshape.491
  11.7 1.9 %convolution_bitcast_fusion = f32[2,16,1,64,64]{3,4,0,1,2:T(8,128)S(1)} fusion(f32[2,64,64,1]{2,1,0,3:T(8,128)} %constant.107, f32[16,64,64]{2,1,0:T(8,128)S(1)} %reshape.491), kind=kOutput, calls=%fused_computation | convolution fusion | flops 100663296 | bytes 819200 | tf_op jit(solution)/shard_map/qkn,afnm->qafkm/dot_general | solution.py:39
  13.6 0.9 multiply_subtract_fusion
  14.5 1.6 %fusion.1 = bf16[2,1,16,32,64]{4,3,0,2,1:T(8,128)(2,1)S(1)} fusion(f32[2,2,32,64,1]{3,2,1,0,4:T(8,128)} %constant.108, f32[1,16,1,64,64]{3,4,0,1,2:T(8,128)S(1)} %get-tuple-element.10, f32[1,16,1,64,64]{3,4,0,1,2:T(8,128)S(1)} %get-tuple-element.9), kind=kOutput, calls=%fused_computation.3 | convolution fusion | flops 100859904 | bytes 688128 | tf_op jit(solution)/shard_map/pqjm,qafkm->pfajk/dot_general | solution.py:47
  16.1 0.2 reshape_reshape.3
  16.3 0.7 copy.54
  17.0 4.2 %all-to-all-start = ((bf16[4,2,16,512]{3,2,1,0:T(8,128)(2,1)}), bf16[4,2,16,512]{3,2,1,0:T(8,128)(2,1)S(1)}, u32[]{:S(2)}, u32[]{:S(2)}) async-start(bf16[4,2,16,512]{3,2,1,0:T(8,128)(2,1)} %bitcast.65), calls=%async_computation | async-start | bytes 262144 | tf_op jit(solution)/shard_map/all_to_all | solution.py:176
  21.2 0.8 reshape.495
  22.1 3.7 %all-to-all-done = bf16[4,2,16,512]{3,2,1,0:T(8,128)(2,1)S(1)} async-done(((bf16[4,2,16,512]{3,2,1,0:T(8,128)(2,1)}), bf16[4,2,16,512]{3,2,1,0:T(8,128)(2,1)S(1)}, u32[]{:S(2)}, u32[]{:S(2)}) %all-to-all-start) | async-done | bytes 131104 | tf_op jit(solution)/shard_map/all_to_all | solution.py:176
  25.8 0.7 copy.32
  26.5 0.8 reshape.493
  27.5 0.6 multiply_add_fusion.2
  28.1 2.2 %add_convert_fusion = bf16[512,128]{1,0:T(8,128)(2,1)S(1)} fusion(f32[512]{0:T(512)S(1)} %bitcast.85, s32[512]{0:T(512)S(1)} %bitcast.80, s32[512]{0:T(512)S(1)} %bitcast.78, f32[512]{0:T(512)S(1)} %bitcast.83), kind=kLoop, calls=%fused_computation.24 | loop fusion | flops 2097152 | bytes 139264 | tf_op jit(solution)/shard_map/convert.2
  30.3 2.2 %select_convert_fusion = bf16[512,128]{1,0:T(8,128)(2,1)S(1)} fusion(f32[512]{0:T(512)S(1)} %bitcast.82, f32[512]{0:T(512)S(1)} %bitcast.86, s32[512]{0:T(512)S(1)} %bitcast.81, s32[512]{0:T(512)S(1)} %bitcast.79, f32[512]{0:T(512)S(1)} %bitcast.84, pred[128]{0:T(512)(128)(4,1)S(1)} %iota_compare_fusion), kind=kLoop, calls=%fused_computation.23 | loop fusion | flops 2162688 | bytes 141440 | tf_op jit(solution)/shard_map/convert.3
  32.6 35.2 %all-gather.2.cloned.1.call-done = bf16[32,2,16,512]{3,2,0,1:T(8,128)(2,1)} async-done(((bf16[4,2,16,512]{3,2,0,1:T(8,128)(2,1)}), bf16[32,2,16,512]{3,2,0,1:T(8,128)(2,1)}) %all-gather.2.cloned.1.call-update) | async-done | bytes 1048592 | tf_op jit(solution)/shard_map/all_gather | solution.py:177
  67.7 2.8 %convert_element_type.111 = f32[32,2,16,512]{3,2,0,1:T(8,128)} convert(bf16[32,2,16,512]{3,2,0,1:T(8,128)(2,1)} %all-gather.2.cloned.1.call-done) | non-fusion elementwise | flops 524288 | bytes 3145728 | tf_op jit(solution)/shard_map/convert_element_type | solution.py:178
  70.6 1.9 %copy.35.s_ref = f32[2,512,512]{2,1,0:T(8,128)S(1)} copy(f32[2,512,512]{1,2,0:T(8,128)} %bitcast.68) | data formatting | bytes 4194304 | tf_op jit(solution)/shard_map/convert_element_type | solution.py:178
  72.5 23.5 %shard_map.122 = (f32[512,32,256]{2,1,0:T(8,128)}, f32[32,256]{1,0:T(8,128)S(1)}) custom-call(f32[2,512,512]{2,1,0:T(8,128)S(1)} %copy.35.s_ref, f32[2,32,512]{2,1,0:T(8,128)S(1)} %pad_maximum_fusion.1.r_ref, bf16[512,256]{1,0:T(8,128)(2,1)S(1)} %pad_maximum_fusion.t_ref, f32[512,32,256]{2,1,0:T(8,128)} %sky_ref.1), custom_call_target="tpu_custom_call" | custom-call | flops 8589934592 | bytes 33554432 | tf_op jit(solution)/shard_map/pallas_call | solution.py:137
  96.0 10.3 %psum.7 = f32[32,256]{1,0:T(8,128)S(1)} all-reduce(f32[32,256]{1,0:T(8,128)S(1)} %get-tuple-element.5), channel_id=1, replica_groups=mesh['grp'=4,'dev'=8] {'grp'}, use_global_device_ids=true, to_apply=%region_0.1 | all-reduce | flops 8192 | bytes 65536 | tf_op jit(solution)/shard_map/psum | solution.py:186
  106.3 0.6 broadcast_multiply_fusion
  (15 shorter events, 0.3 us)
Async XLA Ops:
  17.0 8.8 %all-to-all-start = ((bf16[4,2,16,512]{3,2,1,0:T(8,128)(2,1)}), bf16[4,2,16,512]{3,2,1,0:T(8,128)(2,1)S(1)}, u32[]{:S(2)}, u32[]{:S(2)}) async-start(bf16[4,2,16,512]{3,2,1,0:T(8,128)(2,1)} %bitcast.65), calls=%async_computation | async-start | bytes 262144 | tf_op jit(solution)/shard_map/all_to_all | solution.py:176
  21.2 46.5 %all-gather.2.cloned.1.call-start = ((), (), s32[]{:S(2)}) async-start(), calls=%async_computation.1 | async-start | bytes 1179648 | tf_op jit(solution)/shard_map/all_gather | solution.py:177
Sparse Core Ops, SparseCore 0:
  26.6 41.0 all-gather.1
